TPU v7x, 512 devices: a whole 4x8x8 slice. The times are simulated.
512 devices in a mesh: dp: 128 (over z, y, core), tensor: 4 (over x).
Axes of the slice: x: 4, y: 8, z: 8, core: 2. Of those that a mesh axis runs over, the one named last changes fastest.
Arguments:
- head_output: bfloat16 [49152, 1536], P('dp', 'tensor'), may hold values from -6 to 6
- out_weight: bfloat16 [1536, 1536], P('tensor'), may hold values from -0.15625 to 0.15625
- block_cotangent: bfloat16 [49152, 1536], P('dp'), may hold values from -6 to 6
- error_memory: bfloat16 [128, 1536, 1536], P('dp', 'tensor'), may hold values from -96 to 96
- right_factor: float32 [1536, 64], replicated, may hold values from -0.15625 to 0.15625
- gate_table: bfloat16 [64, 1536], replicated, may hold values from -6 to 6
- sample_weight: float32 [64], replicated, may hold values from 0.5 to 2
- time_bins: int32 [384], P('dp'), may hold values from 0 to 63
- token_loss: float32 [49152], P('dp'), as said below
- loss_bins: int32 [49152], P('dp'), may hold values from 0 to 63
Outputs:
- head_grad: bfloat16 [49152, 1536], P('dp', 'tensor')
- left_basis: float32 [1536, 64], P('tensor')
- new_right: float32 [1536, 64], P('tensor')
- gate_grad: float32 [64, 1536], P(None, 'tensor')
- loss_histogram: float32 [64], replicated
Inputs may be any that keep to these rules, and one draw needn't show every extreme that they name: `token_loss`: positive losses.
All inputs are finite; a program needn't handle non-finite values.
Results may differ from a plain program's by a relative error of at most 0.0049.
Values sent between devices are 32-bit elements; how exact they have to be, the bound alone decides.
A program may use at most 64 MiB of HBM per device.

v0:
```python
import functools
import math

import jax
import jax.numpy as jnp
from jax import lax
from jax.experimental import pallas as pl
from jax.experimental.pallas import tpu as pltpu
from jax.sharding import PartitionSpec as P

MESH = pl.DeviceIdType.MESH
F32 = jnp.float32
BF16 = jnp.bfloat16
HIGHEST = lax.Precision.HIGHEST
NN = (((1,), (0,)), ((), ()))
NT = (((1,), (1,)), ((), ()))


def split(x):
    high = x.astype(BF16)
    low = (x - high.astype(F32)).astype(BF16)
    return jnp.concatenate([high, low], axis=0)


def fold(x):
    half = x.shape[0] // 2
    return x[:half] + x[half:]


def eliminate(ref, begin, end):
    groups, _, width = ref.shape
    sub = lax.broadcasted_iota(jnp.int32, (8, width), 0)

    def wide(x, j):
        return jnp.broadcast_to(x[:, j : j + 1], (8, width))

    def block(k, carry):
        own = ref[k]
        rows = [ref[g] for g in range(groups)]
        for r in range(0, 8, 2):
            first, second = wide(own, r), wide(own, r + 1)
            aa = first[r : r + 1]
            ab = first[r + 1 : r + 2]
            bb = second[r + 1 : r + 2]
            inverse = 1.0 / (aa * bb - ab * ab)
            top = own[r : r + 1]
            low = own[r + 1 : r + 2]
            one = jnp.broadcast_to((bb * inverse) * top - (ab * inverse) * low, (8, width))
            two = jnp.broadcast_to((aa * inverse) * low - (ab * inverse) * top, (8, width))
            if r < 6:
                own = own - jnp.where(sub > r + 1, first * one + second * two, 0.0)
            for g in range(groups):
                change = wide(rows[g], r) * one + wide(rows[g], r + 1) * two
                rows[g] = rows[g] - jnp.where(g > k, change, 0.0)
        for g in range(groups):
            ref[g] = pltpu.roll(jnp.where(g == k, own, rows[g]), width - 8, 1)
        return carry

    lax.fori_loop(begin, end, block, 0)


def unscaled_to_inverse(rows, rank):
    out = []
    width = rows[0].shape[1]
    lane = lax.broadcasted_iota(jnp.int32, (8, width), 1)
    sub = lax.broadcasted_iota(jnp.int32, (8, width), 0)
    odd = lax.rem(sub, 2) == 1
    for g, x in enumerate(rows):
        row = sub + (8 * g + rank)
        before = jnp.concatenate([x[7:], x[:7]], axis=0)
        over = jnp.sum(jnp.where(lane == row - 1, before, 0.0), axis=1, keepdims=True)
        off = jnp.sum(jnp.where(lane == row - 1, x, 0.0), axis=1, keepdims=True)
        x = jnp.where(odd, x - (off / jnp.where(odd[:, :1], over, 1.0)) * before, x)
        diag = jnp.sum(jnp.where(lane == row, x, 0.0), axis=1, keepdims=True)
        out.append(x / jnp.sqrt(diag))
    return jnp.concatenate(out, axis=0)


def far_first(i, n):
    return n // 2 + ((i + 1) // 2) * (1 - 2 * (i % 2))


def each(count, step):
    def body(i, carry):
        step(i)
        return carry

    lax.fori_loop(0, count, body, 0)


def wrap(value, n):
    return jnp.where(value >= n, value - n, value)


A1, TG, A2, A3, G1, G2, G3, GRAM, XX, C4, C5, PAIR = range(12)


def main_kernel(
    n, nx, workers, hist_scale,
    tb_hbm, sw_hbm, head_hbm, weight_hbm, cot_hbm, err_hbm, right_hbm, gate_hbm, loss_hbm, bins_hbm,
    right_o, basis_o, gate_o, hist_o, grad_o,
    tb_ref, sw_ref, head, weight, cot, right, gate, loss, bins, load_sem,
    both_g, head_t, rstack, scale, left_v, stack_v, merged, own_s, sib_s,
    l_src, l_in, l_mid, l_all,
    g_src, g_in, g_mid, g_all,
    s_src, s_in, s_x, s_xin, s_mid, s_all,
    t_src, t_in, gram, chol,
    ssem, rsem,
):
    rank = right.shape[0]
    tokens, feats = head.shape
    width = cot.shape[1]
    latents, per = loss.shape
    nbins = gate.shape[0]
    share = width // nx
    half = rank // 2
    piece = half // n
    pairs = 2 * n
    FIRST = PAIR + nx

    index = lax.axis_index("dp")
    x = lax.axis_index("tensor")
    c = lax.rem(index, 2)
    y = lax.rem(index // 2, n)
    z = index // (2 * n)

    def at_z(j, core):
        return ((j * n + y) * 2 + core, x)

    def at_y(j, core):
        return ((z * n + j) * 2 + core, x)

    a = jnp.where(c == 0, z, y)
    b = jnp.where(c == 0, y, z)

    a_step = jnp.where(c == 0, 2 * n, 2)
    a_base = jnp.where(c == 0, 2 * y, 2 * n * z)
    b_step = jnp.where(c == 0, 2, 2 * n)
    b_base = jnp.where(c == 0, 2 * n * z, 2 * y) + c

    def at_a(j, core):
        return (j * a_step + a_base + core, x)

    def at_b(j):
        return (j * b_step + b_base, x)

    sibling = (index + 1 - 2 * c, x)

    barrier = pltpu.get_barrier_semaphore()

    def greet(device):
        pl.semaphore_signal(barrier, inc=1, device_id=device, device_id_type=MESH)

    @functools.partial(each, n - 1)
    def _(i):
        k = far_first(i, n)
        jz = wrap(z + k, n)
        jy = wrap(y + k, n)
        for core in (0, 1):
            greet(at_z(jz, core))
            greet(at_y(jy, core))

    greet(sibling)

    @functools.partial(each, nx - 1)
    def _(i):
        greet((index, wrap(x + far_first(i, nx), nx)))

    wanted = [(right_hbm, right), (tb_hbm, tb_ref), (sw_hbm, sw_ref), (gate_hbm, gate)]
    for i in range(feats // 128):
        rows = pl.ds(i * 128, 128)
        wanted.append((err_hbm.at[0, rows], both_g.at[rows]))
    for l in range(latents):
        rows = pl.ds(l * per, per)
        wanted.append((cot_hbm.at[rows], cot.at[rows]))
    wanted += [(head_hbm, head), (loss_hbm, loss), (bins_hbm, bins), (weight_hbm, weight)]
    loads = []
    for k, (src, dst) in enumerate(wanted):
        loads.append(pltpu.make_async_copy(src, dst, load_sem.at[k]))
        loads[-1].start()
    e_load = 4
    c_load = e_load + feats // 128
    h_load = c_load + latents

    def remote(src, dst, phase, device):
        return pltpu.make_async_remote_copy(
            src_ref=src, dst_ref=dst, send_sem=ssem.at[phase], recv_sem=rsem.at[phase],
            device_id=device, device_id_type=MESH,
        )

    def scatter_send(src, dst, phase):
        @functools.partial(each, n - 1)
        def _(i):
            k = far_first(i, n)
            jz = wrap(z + k, n)
            jy = wrap(y + k, n)
            remote(src.at[jz], dst.at[z * 2 + c], phase, at_z(jz, 0)).start()
            remote(src.at[n + jy], dst.at[y * 2 + c], phase, at_y(jy, 1)).start()

        @pl.when(c == 1)
        def _():
            remote(src.at[z], dst.at[z * 2 + 1], phase, sibling).start()

        @pl.when(c == 0)
        def _():
            remote(src.at[n + y], dst.at[y * 2], phase, sibling).start()

        dst[a * 2 + c] = src[c * n + a]

    def wait_many(ref, count, phase, recv=True):
        part = ref.at[pl.ds(0, count)]
        copy = remote(part, part, phase, sibling)
        if recv:
            copy.wait_recv()
        else:
            copy.wait_send()

    def sum_slots(ref, count):
        out = ref[0]
        for k in range(1, count):
            out = out + ref[k]
        return out

    def ring_send(ref, phase):
        @functools.partial(each, n - 1)
        def _(i):
            remote(ref.at[b], ref.at[b], phase, at_b(wrap(b + far_first(i, n), n))).start()

    def gather_send(ref, phase):
        mine = c * n + a

        @functools.partial(each, n - 1)
        def _(i):
            j = wrap(a + far_first(i, n), n)
            for core in (0, 1):
                remote(ref.at[mine], ref.at[mine], phase, at_a(j, core)).start()

        remote(ref.at[mine], ref.at[mine], phase, sibling).start()

    loads[0].wait()
    rstack[...] = split(right[...])

    @functools.partial(each, feats // 128)
    def _(i):
        rows = pl.ds(pl.multiple_of(i * 128, 128), 128)
        pltpu.make_async_copy(err_hbm.at[0, rows], both_g.at[rows], load_sem.at[e_load + i]).wait()
        term = lax.dot_general(both_g[rows, :], rstack[...], NT, preferred_element_type=F32)
        left_v[:, rows] = fold(term.T)

    for k in (1, 2, 3):
        loads[k].wait()
    bin_of = lax.broadcasted_iota(jnp.int32, (8, nbins), 1)
    row_of = lax.broadcasted_iota(jnp.int32, (8, nbins), 0)
    onehot = jnp.zeros((8, nbins), F32)
    weights = []
    for l in range(latents):
        tb = tb_ref[l]
        weights.append(sw_ref[tb])
        onehot = jnp.where((row_of == l) & (bin_of == tb), 1.0, onehot)
    gates = lax.dot_general(onehot.astype(BF16), gate[...], NN, preferred_element_type=F32)
    row8 = lax.broadcasted_iota(jnp.int32, (8, width), 0)
    lat8 = jnp.zeros((8, width), F32)
    for l in range(latents):
        lat8 = jnp.where(row8 == l, weights[l], lat8)
    scale[...] = gates * lat8
    loads[h_load].wait()

    @functools.partial(each, latents)
    def _(l):
        rows = pl.ds(pl.multiple_of(l * per, per), per)
        pltpu.make_async_copy(cot_hbm.at[rows], cot.at[rows], load_sem.at[c_load + l]).wait()
        part = (cot[rows, :].astype(F32) * scale[pl.ds(l, 1), :]).astype(BF16)
        both_g[pl.ds(pl.multiple_of(feats + l * per, per), per), :] = part
        mixed = fold(lax.dot_general(part, rstack[...], NT, preferred_element_type=F32).T)
        left_v[...] += fold(lax.dot_general(split(mixed), head[rows, :], NN, preferred_element_type=F32))

    left = left_v[...]
    for k in range(pairs):
        l_src[k] = left[k * piece : (k + 1) * piece]

    pl.semaphore_wait(barrier, 4 * (n - 1) + 1 + (nx - 1))
    scatter_send(l_src, l_in, A1)

    loads[h_load + 3].wait()
    row_s = lax.broadcasted_iota(jnp.int32, (8, share), 0)

    @functools.partial(each, nx)
    def _(t):
        cols = pl.ds(pl.multiple_of(t * share, 128), share)
        out = jnp.zeros((8, share), F32)
        for l in range(latents):
            rows = pl.ds(l * per, per)
            branch = lax.dot_general(head[rows, :], weight[:, cols], NN, preferred_element_type=F32)
            row = jnp.sum(branch * cot[rows, cols].astype(F32), axis=0, keepdims=True) * weights[l]
            out = jnp.where(row_s == l, row, out)
        t_src[t] = out

    stack_v[rank:, feats:] = jnp.zeros((rank, feats), BF16)
    t_in[x] = t_src[x]

    @functools.partial(each, nx - 1)
    def _(i):
        j = wrap(x + far_first(i, nx), nx)
        remote(t_src.at[j], t_in.at[x], TG, (index, j)).start()

    wait_many(l_in, pairs - 1, A1)
    l_mid[b] = sum_slots(l_in, pairs)
    ring_send(l_mid, A2)

    head_t[...] = head[...].T

    @functools.partial(each, nx)
    def _(t):
        cols = pl.ds(pl.multiple_of(t * share, 128), share)
        for i in range(feats // 128):
            rows = pl.ds(i * 128, 128)
            whole = lax.dot_general(head_t[rows, :], both_g[feats:, cols], NN, preferred_element_type=F32)
            whole = whole + both_g[rows, cols].astype(F32)
            high = whole.astype(BF16)
            merged[rows, cols] = high
            merged[pl.ds(feats + i * 128, 128), cols] = (whole - high.astype(F32)).astype(BF16)

    loads[h_load + 1].wait()
    loads[h_load + 2].wait()
    bin_row = lax.broadcasted_iota(jnp.int32, (nbins, per), 0)
    hist = jnp.zeros((nbins, per), F32)
    for l in range(latents):
        hist = hist + jnp.where(bin_row == bins[l : l + 1, :], weights[l] * loss[l : l + 1, :], 0.0)
    wait_many(t_in, nx - 1, TG)
    lat_sum = sum_slots(t_in, nx)
    bin_s = lax.broadcasted_iota(jnp.int32, (nbins, share), 0)
    spread = jnp.zeros((nbins, share), F32)
    for l in range(latents):
        spread = spread + jnp.where(bin_s == tb_ref[l], lat_sum[l : l + 1, :], 0.0)
    for k in range(pairs):
        g_src[k, :, share:] = hist[k * piece : (k + 1) * piece]
        g_src[k, :, :share] = spread[k * piece : (k + 1) * piece]
    scatter_send(g_src, g_in, G1)

    wait_many(l_mid, n - 1, A2)
    l_all[c * n + a] = sum_slots(l_mid, n) * (1.0 / workers)
    gather_send(l_all, A3)

    @functools.partial(each, latents)
    def _(l):
        grad_o[pl.ds(pl.multiple_of(l * per, per), per), :] = lax.dot_general(
            both_g[pl.ds(pl.multiple_of(feats + l * per, per), per), :], weight[...], NT, preferred_element_type=F32
        ).astype(BF16)

    wait_many(g_in, pairs - 1, G1)
    g_mid[b] = sum_slots(g_in, pairs)
    ring_send(g_mid, G2)

    wait_many(l_all, pairs - 1, A3)
    left = jnp.concatenate([l_all[k] for k in range(pairs)], axis=0)
    high = left.astype(BF16)
    low = (left - high.astype(F32)).astype(BF16)
    stack_v[:rank, :feats] = high
    stack_v[:rank, feats:] = high
    stack_v[rank:, :feats] = low

    def target(i):
        return wrap(x + far_first(i, nx), nx)

    def part_start(i):
        cols = pl.ds(pl.multiple_of(target(i) * share, 128), share)
        term = fold(lax.dot_general(stack_v[...], merged[:, cols], NN, preferred_element_type=F32))
        own_s[i, 0] = term[:half]
        own_s[i, 1] = term[half:]
        remote(own_s.at[i, 1 - c], sib_s.at[i], PAIR + i, sibling).start()

    def part_scatter(i):
        remote(sib_s.at[i], sib_s.at[i], PAIR + i, sibling).wait_recv()
        total = own_s[i, c] + sib_s[i]
        for k in range(n):
            s_src[i, k] = total[k * piece : (k + 1) * piece]
        s_in[i, a] = s_src[i, a]

        @functools.partial(each, n - 1)
        def _(k):
            j = wrap(a + far_first(k, n), n)
            remote(s_src.at[i, j], s_in.at[i, a], FIRST + i, at_a(j, c)).start()

    def part_sum(i):
        wait_many(s_in.at[i], n - 1, FIRST + i)
        total = s_in[i, 0]
        for k in range(1, n):
            total = total + s_in[i, k]
        return total

    lead = min(nx, 2)

    @functools.partial(each, nx + lead)
    def _(i):
        @pl.when(i < nx)
        def _():
            part_start(i)

        @pl.when(i >= lead)
        def _():
            part_scatter(i - lead)

    padded = jnp.concatenate([left, jnp.zeros((128 - rank, share), F32)], axis=0)
    gram[x] = lax.dot_general(left, padded, NT, precision=HIGHEST, preferred_element_type=F32)

    @functools.partial(each, nx - 1)
    def _(i):
        remote(gram.at[x], gram.at[x], GRAM, (index, target(i))).start()

    wait_many(g_mid, n - 1, G2)
    g_all[c * n + a] = sum_slots(g_mid, n)
    gather_send(g_all, G3)

    @functools.partial(each, nx - 1)
    def _(i):
        s_x[i] = part_sum(i)
        remote(s_x.at[i], s_xin.at[x], XX, (index, target(i))).start()

    groups = rank // 8
    wait_many(gram, nx - 1, GRAM)
    whole = sum_slots(gram, nx)
    eye_r = lax.broadcasted_iota(jnp.int32, (rank, 128), 0)
    eye_c = lax.broadcasted_iota(jnp.int32, (rank, 128), 1)
    whole = jnp.where(eye_c == eye_r + rank, 1.0, whole)
    for g in range(groups):
        chol[g] = whole[8 * g : 8 * g + 8]
    eliminate(chol, 0, groups // 4)
    s_xin[x] = part_sum(nx - 1)

    wait_many(s_xin, nx - 1, XX)
    s_mid[b] = sum_slots(s_xin, nx)
    ring_send(s_mid, C4)

    eliminate(chol, groups // 4, 5 * groups // 8)

    wait_many(s_mid, n - 1, C4)
    s_all[c * n + a] = sum_slots(s_mid, n)
    gather_send(s_all, C5)
    eliminate(chol, 5 * groups // 8, groups)
    inverse = unscaled_to_inverse([chol[g] for g in range(groups)], rank)[:, :rank]
    basis_o[...] = lax.dot_general(inverse, left, NN, precision=HIGHEST, preferred_element_type=F32)
    wait_many(g_all, pairs - 1, G3)
    gates = jnp.concatenate([g_all[k] for k in range(pairs)], axis=0)
    gate_o[...] = gates[:, :share]
    hist_o[...] = jnp.sum(gates[:, share:], axis=1, keepdims=True).T * hist_scale
    inv_high = inverse.astype(BF16)
    inv_low = (inverse - inv_high.astype(F32)).astype(BF16)
    inv_stack = jnp.concatenate([inv_high, inv_high, inv_low], axis=1)

    wait_many(l_src, pairs - 1, A1, False)
    wait_many(t_src, nx - 1, TG, False)
    wait_many(l_mid, n - 1, A2, False)
    wait_many(l_all, pairs - 1, A3, False)
    wait_many(g_src, pairs - 1, G1, False)

    @functools.partial(each, nx)
    def _(i):
        remote(sib_s.at[i], sib_s.at[i], PAIR + i, sibling).wait_send()
        wait_many(s_src.at[i], n - 1, FIRST + i, False)

    wait_many(gram, nx - 1, GRAM, False)
    wait_many(g_mid, n - 1, G2, False)
    wait_many(s_x, nx - 1, XX, False)
    wait_many(s_mid, n - 1, C4, False)
    wait_many(g_all, pairs - 1, G3, False)

    wait_many(s_all, pairs - 1, C5)
    s_whole = jnp.concatenate([s_all[k] for k in range(pairs)], axis=0)
    s_high = s_whole.astype(BF16)
    s_low = (s_whole - s_high.astype(F32)).astype(BF16)
    right_o[...] = lax.dot_general(
        inv_stack, jnp.concatenate([s_high, s_low, s_high], axis=0), NN, preferred_element_type=F32
    ) * (1.0 / workers)
    wait_many(s_all, pairs - 1, C5, False)


def end_kernel(*refs):
    count = len(refs) // 2
    sem = refs[-1]
    copies = [pltpu.make_async_copy(refs[k], refs[count + k], sem.at[k]) for k in range(count)]
    for copy in copies:
        copy.start()
    for copy in copies:
        copy.wait()


def per_device(n, nx, head, weight, cot, err, right, gate, sample, tbins, loss, lbins):
    workers = 2 * n * n
    rank = right.shape[1]
    tokens, feats = head.shape
    width = cot.shape[1]
    latents = tbins.shape[0]
    per = tokens // latents
    nbins = gate.shape[0]
    share = width // nx
    half = rank // 2
    piece = half // n
    pairs = 2 * n
    gwidth = share + per
    vmem = pl.BlockSpec(memory_space=pltpu.VMEM)
    hbm = pl.BlockSpec(memory_space=pltpu.HBM)
    V = pltpu.VMEM
    DMA = pltpu.SemaphoreType.DMA
    out = jax.ShapeDtypeStruct
    operands = (
        tbins, sample, head, weight, cot, err, right.T, gate,
        loss.reshape(latents, per), lbins.reshape(latents, per),
    )
    kinds = (
        ((rank, share), F32),
        ((rank, share), F32),
        ((nbins, share), F32),
        ((1, nbins), F32),
        ((tokens, feats), BF16),
    )
    results = pl.pallas_call(
        functools.partial(main_kernel, n, nx, workers, nbins / (tokens * workers)),
        out_shape=tuple(V(shape, dtype) for shape, dtype in kinds),
        in_specs=[hbm] * 10,
        out_specs=(vmem,) * 5,
        scratch_shapes=[
            pltpu.SMEM(tbins.shape, jnp.int32),
            pltpu.SMEM(sample.shape, F32),
            V(head.shape, BF16),
            V(weight.shape, BF16),
            V(cot.shape, BF16),
            V((rank, width), F32),
            V(gate.shape, BF16),
            V((latents, per), F32),
            V((latents, per), jnp.int32),
            DMA((8 + feats // 128 + latents,)),
            V((feats + tokens, width), BF16),
            V((feats, tokens), BF16),
            V((2 * rank, width), BF16),
            V((8, width), F32),
            V((rank, share), F32),
            V((2 * rank, 2 * feats), BF16),
            V((2 * feats, width), BF16),
            V((nx, 2, half, share), F32),
            V((nx, half, share), F32),
            V((pairs, piece, share), F32),
            V((pairs, piece, share), F32),
            V((n, piece, share), F32),
            V((pairs, piece, share), F32),
            V((pairs, piece, gwidth), F32),
            V((pairs, piece, gwidth), F32),
            V((n, piece, gwidth), F32),
            V((pairs, piece, gwidth), F32),
            V((nx, n, piece, share), F32),
            V((nx, n, piece, share), F32),
            V((nx, piece, share), F32),
            V((nx, piece, share), F32),
            V((n, piece, share), F32),
            V((pairs, piece, share), F32),
            V((nx, 8, share), F32),
            V((nx, 8, share), F32),
            V((nx, rank, 128), F32),
            V((rank // 8, 8, 128), F32),
            DMA((PAIR + 2 * nx,)),
            DMA((PAIR + 2 * nx,)),
        ],
        compiler_params=pltpu.CompilerParams(
            collective_id=0, has_side_effects=True, vmem_limit_bytes=32 * 1024 * 1024
        ),
        name="main",
    )(*[pltpu.with_memory_space_constraint(v, pltpu.HBM) for v in operands])
    new_right, basis, gate_grad, hist, grad = pl.pallas_call(
        end_kernel,
        out_shape=tuple(out(shape, dtype) for shape, dtype in kinds),
        in_specs=[vmem] * 5,
        out_specs=(hbm,) * 5,
        scratch_shapes=[DMA((5,))],
        compiler_params=pltpu.CompilerParams(vmem_limit_bytes=8 * 1024 * 1024),
        name="finish",
    )(*results)
    return grad, basis.T, new_right.T, gate_grad, hist.reshape(nbins)


def solution(mesh):
    n = math.isqrt(mesh.shape["dp"] // 2)
    assert 2 * n * n == mesh.shape["dp"]
    placed = (
        P("dp", "tensor"),
        P("tensor", None),
        P("dp", None),
        P("dp", "tensor", None),
        P(),
        P(),
        P(),
        P("dp"),
        P("dp"),
        P("dp"),
    )
    return jax.shard_map(
        functools.partial(per_device, n, mesh.shape["tensor"]),
        mesh=mesh,
        in_specs=placed,
        out_specs=(P("dp", "tensor"), P("tensor", None), P("tensor", None), P(None, "tensor"), P()),
        check_vma=False,
    )
```

profile of v0, /device:TPU:1, one launch (start us, length us, event | category | flops | bytes accessed | tf_op | source)
XLA Modules:
  0.0 50.3 jit_solution(7964481156497289672)
XLA Ops:
  0.6 48.8 %main.1 = (f32[64,384]{1,0:T(8,128)S(1)}, f32[64,384]{1,0:T(8,128)S(1)}, f32[64,384]{1,0:T(8,128)S(1)}, f32[1,64]{1,0:T(1,128)S(1)}, bf16[384,384]{1,0:T(8,128)(2,1)S(1)}) custom-call(s32[3]{0:T(128)} %tb_hbm.1, f32[64]{0:T(128)} %sw_hbm.1, bf16[384,384]{1,0:T(8,128)(2,1)} %head_hbm.1, bf16[384,1536]{1,0:T(8,128)(2,1)} %weight_hbm.1, ...), custom_call_target="tpu_custom_call" | custom-call | tf_op jit(solution)/shard_map/main/pallas_call | solution.py:516
  49.4 0.9 %finish.1 = (f32[64,384]{1,0:T(8,128)}, f32[64,384]{1,0:T(8,128)}, f32[64,384]{1,0:T(8,128)}, f32[1,64]{1,0:T(1,128)}, bf16[384,384]{1,0:T(8,128)(2,1)}) custom-call(f32[64,384]{1,0:T(8,128)S(1)} %get-tuple-element.15.refs_0_, f32[64,384]{1,0:T(8,128)S(1)} %get-tuple-element.16.refs_1_, f32[64,384]{1,0:T(8,128)S(1)} %get-tuple-element.17.refs_2_, ...), custom_call_target="tpu_custom_call" | custom-call | tf_op jit(solution)/shard_map/finish/pallas_call | solution.py:567
where the time goes:
time: 50.4 us; the launch traced here: 50.3 us
  Pallas kernels  49.6 us (98%)
  between operations  0.64 us (1%)
    pallas_call x1, Pallas kernels, per_device(): pl.pallas_call(functools.partial(main_kernel, n, nx, workers, nbins / (to...  48.8 us

commit v1 on v0

--- a/solution.py
+++ b/solution.py
@@ -92,7 +92,7 @@
     return jnp.where(value >= n, value - n, value)
 
 
-A1, TG, A2, A3, G1, G2, G3, GRAM, XX, C4, C5, PAIR = range(12)
+A1, TG, A2, A3, G1, G2, G3, GRAM, XX, C5, PAIR = range(11)
 
 
 def main_kernel(
@@ -103,7 +103,7 @@
     both_g, head_t, rstack, scale, left_v, stack_v, merged, own_s, sib_s,
     l_src, l_in, l_mid, l_all,
     g_src, g_in, g_mid, g_all,
-    s_src, s_in, s_x, s_xin, s_mid, s_all,
+    s_src, s_in, s_x, s_xin, s_all,
     t_src, t_in, gram, chol,
     ssem, rsem,
 ):
@@ -141,8 +141,8 @@
     def at_a(j, core):
         return (j * a_step + a_base + core, x)
 
-    def at_b(j):
-        return (j * b_step + b_base, x)
+    def at_b(j, t=x):
+        return (j * b_step + b_base, t)
 
     sibling = (index + 1 - 2 * c, x)
 
@@ -414,7 +414,11 @@
     @functools.partial(each, nx - 1)
     def _(i):
         s_x[i] = part_sum(i)
-        remote(s_x.at[i], s_xin.at[x], XX, (index, target(i))).start()
+
+        @functools.partial(each, n)
+        def _(k):
+            j = wrap(b + far_first(k, n), n)
+            remote(s_x.at[i], s_xin.at[x * n + b], XX, at_b(j, target(i))).start()
 
     groups = rank // 8
     wait_many(gram, nx - 1, GRAM)
@@ -425,16 +429,18 @@
     for g in range(groups):
         chol[g] = whole[8 * g : 8 * g + 8]
     eliminate(chol, 0, groups // 4)
-    s_xin[x] = part_sum(nx - 1)
-
-    wait_many(s_xin, nx - 1, XX)
-    s_mid[b] = sum_slots(s_xin, nx)
-    ring_send(s_mid, C4)
+    s_x[nx - 1] = part_sum(nx - 1)
+    s_xin[x * n + b] = s_x[nx - 1]
+
+    @functools.partial(each, n - 1)
+    def _(k):
+        j = wrap(b + far_first(k, n), n)
+        remote(s_x.at[nx - 1], s_xin.at[x * n + b], XX, at_b(j)).start()
 
     eliminate(chol, groups // 4, 5 * groups // 8)
 
-    wait_many(s_mid, n - 1, C4)
-    s_all[c * n + a] = sum_slots(s_mid, n)
+    wait_many(s_xin, nx * n - 1, XX)
+    s_all[c * n + a] = sum_slots(s_xin, nx * n)
     gather_send(s_all, C5)
     eliminate(chol, 5 * groups // 8, groups)
     inverse = unscaled_to_inverse([chol[g] for g in range(groups)], rank)[:, :rank]
@@ -460,8 +466,7 @@
 
     wait_many(gram, nx - 1, GRAM, False)
     wait_many(g_mid, n - 1, G2, False)
-    wait_many(s_x, nx - 1, XX, False)
-    wait_many(s_mid, n - 1, C4, False)
+    wait_many(s_xin, nx * n - 1, XX, False)
     wait_many(g_all, pairs - 1, G3, False)
 
     wait_many(s_all, pairs - 1, C5)
@@ -549,8 +554,7 @@
             V((nx, n, piece, share), F32),
             V((nx, n, piece, share), F32),
             V((nx, piece, share), F32),
-            V((nx, piece, share), F32),
-            V((n, piece, share), F32),
+            V((nx * n, piece, share), F32),
             V((pairs, piece, share), F32),
             V((nx, 8, share), F32),
             V((nx, 8, share), F32),

time: 50.4 us -> 49.3 us (0.978)
  Pallas kernels: 49.6 us -> 48.5 us
    pallas_call x1, Pallas kernels: 48.8 us -> 47.7 us  [per_device(): pl.pallas_call(functools.partial(main_kernel, n, nx, workers, nbins / (to...]
where the time goes in v1:
time: 49.3 us; the launch traced here: 49.2 us
  Pallas kernels  48.5 us (98%)
  between operations  0.64 us (1%)
    pallas_call x1, Pallas kernels, per_device(): pl.pallas_call(functools.partial(main_kernel, n, nx, workers, nbins / (to...  47.7 us

profile of v1, /device:TPU:1, one launch (start us, length us, event | category | flops | bytes accessed | tf_op | source)
XLA Modules:
  0.0 49.2 jit_solution(15821634435084295991)
XLA Ops:
  0.6 47.7 %main.1 = (f32[64,384]{1,0:T(8,128)S(1)}, f32[64,384]{1,0:T(8,128)S(1)}, f32[64,384]{1,0:T(8,128)S(1)}, f32[1,64]{1,0:T(1,128)S(1)}, bf16[384,384]{1,0:T(8,128)(2,1)S(1)}) custom-call(s32[3]{0:T(128)} %tb_hbm.1, f32[64]{0:T(128)} %sw_hbm.1, bf16[384,384]{1,0:T(8,128)(2,1)} %head_hbm.1, bf16[384,1536]{1,0:T(8,128)(2,1)} %weight_hbm.1, ...), custom_call_target="tpu_custom_call" | custom-call | tf_op jit(solution)/shard_map/main/pallas_call | solution.py:521
  48.3 0.9 %finish.1 = (f32[64,384]{1,0:T(8,128)}, f32[64,384]{1,0:T(8,128)}, f32[64,384]{1,0:T(8,128)}, f32[1,64]{1,0:T(1,128)}, bf16[384,384]{1,0:T(8,128)(2,1)}) custom-call(f32[64,384]{1,0:T(8,128)S(1)} %get-tuple-element.15.refs_0_, f32[64,384]{1,0:T(8,128)S(1)} %get-tuple-element.16.refs_1_, f32[64,384]{1,0:T(8,128)S(1)} %get-tuple-element.17.refs_2_, ...), custom_call_target="tpu_custom_call" | custom-call | tf_op jit(solution)/shard_map/finish/pallas_call | solution.py:571

commit v2 on v1

--- a/solution.py
+++ b/solution.py
@@ -92,7 +92,7 @@
     return jnp.where(value >= n, value - n, value)
 
 
-A1, TG, A2, A3, G1, G2, G3, GRAM, XX, C5, PAIR = range(11)
+A1, TG, A2, A3, G1, G2, G3, GRAM, XX, C5, FIRST = range(11)
 
 
 def main_kernel(
@@ -100,7 +100,7 @@
     tb_hbm, sw_hbm, head_hbm, weight_hbm, cot_hbm, err_hbm, right_hbm, gate_hbm, loss_hbm, bins_hbm,
     right_o, basis_o, gate_o, hist_o, grad_o,
     tb_ref, sw_ref, head, weight, cot, right, gate, loss, bins, load_sem,
-    both_g, head_t, rstack, scale, left_v, stack_v, merged, own_s, sib_s,
+    both_g, head_t, rstack, scale, left_v, stack_v, merged,
     l_src, l_in, l_mid, l_all,
     g_src, g_in, g_mid, g_all,
     s_src, s_in, s_x, s_xin, s_all,
@@ -116,7 +116,6 @@
     half = rank // 2
     piece = half // n
     pairs = 2 * n
-    FIRST = PAIR + nx
 
     index = lax.axis_index("dp")
     x = lax.axis_index("tensor")
@@ -362,43 +361,20 @@
     def target(i):
         return wrap(x + far_first(i, nx), nx)
 
-    def part_start(i):
+    @functools.partial(each, nx)
+    def _(i):
         cols = pl.ds(pl.multiple_of(target(i) * share, 128), share)
         term = fold(lax.dot_general(stack_v[...], merged[:, cols], NN, preferred_element_type=F32))
-        own_s[i, 0] = term[:half]
-        own_s[i, 1] = term[half:]
-        remote(own_s.at[i, 1 - c], sib_s.at[i], PAIR + i, sibling).start()
-
-    def part_scatter(i):
-        remote(sib_s.at[i], sib_s.at[i], PAIR + i, sibling).wait_recv()
-        total = own_s[i, c] + sib_s[i]
-        for k in range(n):
-            s_src[i, k] = total[k * piece : (k + 1) * piece]
-        s_in[i, a] = s_src[i, a]
-
-        @functools.partial(each, n - 1)
-        def _(k):
-            j = wrap(a + far_first(k, n), n)
-            remote(s_src.at[i, j], s_in.at[i, a], FIRST + i, at_a(j, c)).start()
+        for k in range(pairs):
+            s_src[i, k] = term[k * piece : (k + 1) * piece]
+        scatter_send(s_src.at[i], s_in.at[i], FIRST + i)
 
     def part_sum(i):
-        wait_many(s_in.at[i], n - 1, FIRST + i)
+        wait_many(s_in.at[i], pairs - 1, FIRST + i)
         total = s_in[i, 0]
-        for k in range(1, n):
+        for k in range(1, pairs):
             total = total + s_in[i, k]
         return total
-
-    lead = min(nx, 2)
-
-    @functools.partial(each, nx + lead)
-    def _(i):
-        @pl.when(i < nx)
-        def _():
-            part_start(i)
-
-        @pl.when(i >= lead)
-        def _():
-            part_scatter(i - lead)
 
     padded = jnp.concatenate([left, jnp.zeros((128 - rank, share), F32)], axis=0)
     gram[x] = lax.dot_general(left, padded, NT, precision=HIGHEST, preferred_element_type=F32)
@@ -461,8 +437,7 @@
 
     @functools.partial(each, nx)
     def _(i):
-        remote(sib_s.at[i], sib_s.at[i], PAIR + i, sibling).wait_send()
-        wait_many(s_src.at[i], n - 1, FIRST + i, False)
+        wait_many(s_src.at[i], pairs - 1, FIRST + i, False)
 
     wait_many(gram, nx - 1, GRAM, False)
     wait_many(g_mid, n - 1, G2, False)
@@ -541,8 +516,6 @@
             V((rank, share), F32),
             V((2 * rank, 2 * feats), BF16),
             V((2 * feats, width), BF16),
-            V((nx, 2, half, share), F32),
-            V((nx, half, share), F32),
             V((pairs, piece, share), F32),
             V((pairs, piece, share), F32),
             V((n, piece, share), F32),
@@ -551,8 +524,8 @@
             V((pairs, piece, gwidth), F32),
             V((n, piece, gwidth), F32),
             V((pairs, piece, gwidth), F32),
-            V((nx, n, piece, share), F32),
-            V((nx, n, piece, share), F32),
+            V((nx, pairs, piece, share), F32),
+            V((nx, pairs, piece, share), F32),
             V((nx, piece, share), F32),
             V((nx * n, piece, share), F32),
             V((pairs, piece, share), F32),
@@ -560,8 +533,8 @@
             V((nx, 8, share), F32),
             V((nx, rank, 128), F32),
             V((rank // 8, 8, 128), F32),
-            DMA((PAIR + 2 * nx,)),
-            DMA((PAIR + 2 * nx,)),
+            DMA((FIRST + nx,)),
+            DMA((FIRST + nx,)),
         ],
         compiler_params=pltpu.CompilerParams(
             collective_id=0, has_side_effects=True, vmem_limit_bytes=32 * 1024 * 1024

time: 49.3 us -> 49 us (level)
  no operation moved by 1% of the time
where the time goes in v2:
time: 49 us; the launch traced here: 48.9 us
  Pallas kernels  48.3 us (99%)
  between operations  0.64 us (1%)
    pallas_call x1, Pallas kernels, per_device(): pl.pallas_call(functools.partial(main_kernel, n, nx, workers, nbins / (to...  47.4 us

profile of v2, /device:TPU:1, one launch (start us, length us, event | category | flops | bytes accessed | tf_op | source)
XLA Modules:
  0.0 48.9 jit_solution(17318464802996317205)
XLA Ops:
  0.6 47.4 %main.1 = (f32[64,384]{1,0:T(8,128)S(1)}, f32[64,384]{1,0:T(8,128)S(1)}, f32[64,384]{1,0:T(8,128)S(1)}, f32[1,64]{1,0:T(1,128)S(1)}, bf16[384,384]{1,0:T(8,128)(2,1)S(1)}) custom-call(s32[3]{0:T(128)} %tb_hbm.1, f32[64]{0:T(128)} %sw_hbm.1, bf16[384,384]{1,0:T(8,128)(2,1)} %head_hbm.1, bf16[384,1536]{1,0:T(8,128)(2,1)} %weight_hbm.1, ...), custom_call_target="tpu_custom_call" | custom-call | tf_op jit(solution)/shard_map/main/pallas_call | solution.py:496
  48.1 0.9 %finish.1 = (f32[64,384]{1,0:T(8,128)}, f32[64,384]{1,0:T(8,128)}, f32[64,384]{1,0:T(8,128)}, f32[1,64]{1,0:T(1,128)}, bf16[384,384]{1,0:T(8,128)(2,1)}) custom-call(f32[64,384]{1,0:T(8,128)S(1)} %get-tuple-element.15.refs_0_, f32[64,384]{1,0:T(8,128)S(1)} %get-tuple-element.16.refs_1_, f32[64,384]{1,0:T(8,128)S(1)} %get-tuple-element.17.refs_2_, ...), custom_call_target="tpu_custom_call" | custom-call | tf_op jit(solution)/shard_map/finish/pallas_call | solution.py:544

commit v3 on v1

--- a/solution.py
+++ b/solution.py
@@ -388,18 +388,7 @@
             total = total + s_in[i, k]
         return total
 
-    lead = min(nx, 2)
-
-    @functools.partial(each, nx + lead)
-    def _(i):
-        @pl.when(i < nx)
-        def _():
-            part_start(i)
-
-        @pl.when(i >= lead)
-        def _():
-            part_scatter(i - lead)
-
+    each(nx, part_start)
     padded = jnp.concatenate([left, jnp.zeros((128 - rank, share), F32)], axis=0)
     gram[x] = lax.dot_general(left, padded, NT, precision=HIGHEST, preferred_element_type=F32)
 
@@ -407,9 +396,8 @@
     def _(i):
         remote(gram.at[x], gram.at[x], GRAM, (index, target(i))).start()
 
-    wait_many(g_mid, n - 1, G2)
-    g_all[c * n + a] = sum_slots(g_mid, n)
-    gather_send(g_all, G3)
+    each(nx, part_scatter)
+
 
     @functools.partial(each, nx - 1)
     def _(i):
@@ -437,6 +425,9 @@
         j = wrap(b + far_first(k, n), n)
         remote(s_x.at[nx - 1], s_xin.at[x * n + b], XX, at_b(j)).start()
 
+    wait_many(g_mid, n - 1, G2)
+    g_all[c * n + a] = sum_slots(g_mid, n)
+    gather_send(g_all, G3)
     eliminate(chol, groups // 4, 5 * groups // 8)
 
     wait_many(s_xin, nx * n - 1, XX)

time: 49.3 us -> 49.1 us (level)
  no operation moved by 1% of the time
where the time goes in v3:
time: 49.1 us; the launch traced here: 49 us
  Pallas kernels  48.4 us (99%)
  between operations  0.64 us (1%)
    pallas_call x1, Pallas kernels, per_device(): pl.pallas_call(functools.partial(main_kernel, n, nx, workers, nbins / (to...  47.5 us

profile of v3, /device:TPU:1, one launch (start us, length us, event | category | flops | bytes accessed | tf_op | source)
XLA Modules:
  0.0 49.0 jit_solution(17360279455881306813)
XLA Ops:
  0.6 47.5 %main.1 = (f32[64,384]{1,0:T(8,128)S(1)}, f32[64,384]{1,0:T(8,128)S(1)}, f32[64,384]{1,0:T(8,128)S(1)}, f32[1,64]{1,0:T(1,128)S(1)}, bf16[384,384]{1,0:T(8,128)(2,1)S(1)}) custom-call(s32[3]{0:T(128)} %tb_hbm.1, f32[64]{0:T(128)} %sw_hbm.1, bf16[384,384]{1,0:T(8,128)(2,1)} %head_hbm.1, bf16[384,1536]{1,0:T(8,128)(2,1)} %weight_hbm.1, ...), custom_call_target="tpu_custom_call" | custom-call | tf_op jit(solution)/shard_map/main/pallas_call | solution.py:512
  48.1 0.9 %finish.1 = (f32[64,384]{1,0:T(8,128)}, f32[64,384]{1,0:T(8,128)}, f32[64,384]{1,0:T(8,128)}, f32[1,64]{1,0:T(1,128)}, bf16[384,384]{1,0:T(8,128)(2,1)}) custom-call(f32[64,384]{1,0:T(8,128)S(1)} %get-tuple-element.15.refs_0_, f32[64,384]{1,0:T(8,128)S(1)} %get-tuple-element.16.refs_1_, f32[64,384]{1,0:T(8,128)S(1)} %get-tuple-element.17.refs_2_, ...), custom_call_target="tpu_custom_call" | custom-call | tf_op jit(solution)/shard_map/finish/pallas_call | solution.py:562

commit v4 on v3

--- a/solution.py
+++ b/solution.py
@@ -27,8 +27,9 @@
     return x[:half] + x[half:]
 
 
-def eliminate(ref, begin, end):
+def eliminate(ref, begin, end, low_group):
     groups, _, width = ref.shape
+    active = range(low_group, groups)
     sub = lax.broadcasted_iota(jnp.int32, (8, width), 0)
 
     def wide(x, j):
@@ -36,7 +37,7 @@
 
     def block(k, carry):
         own = ref[k]
-        rows = [ref[g] for g in range(groups)]
+        rows = {g: ref[g] for g in active}
         for r in range(0, 8, 2):
             first, second = wide(own, r), wide(own, r + 1)
             aa = first[r : r + 1]
@@ -49,10 +50,10 @@
             two = jnp.broadcast_to((aa * inverse) * low - (ab * inverse) * top, (8, width))
             if r < 6:
                 own = own - jnp.where(sub > r + 1, first * one + second * two, 0.0)
-            for g in range(groups):
+            for g in active:
                 change = wide(rows[g], r) * one + wide(rows[g], r + 1) * two
                 rows[g] = rows[g] - jnp.where(g > k, change, 0.0)
-        for g in range(groups):
+        for g in active:
             ref[g] = pltpu.roll(jnp.where(g == k, own, rows[g]), width - 8, 1)
         return carry
 
@@ -408,6 +409,17 @@
             j = wrap(b + far_first(k, n), n)
             remote(s_x.at[i], s_xin.at[x * n + b], XX, at_b(j, target(i))).start()
 
+    s_x[nx - 1] = part_sum(nx - 1)
+    s_xin[x * n + b] = s_x[nx - 1]
+
+    @functools.partial(each, n - 1)
+    def _(k):
+        j = wrap(b + far_first(k, n), n)
+        remote(s_x.at[nx - 1], s_xin.at[x * n + b], XX, at_b(j)).start()
+
+    wait_many(g_mid, n - 1, G2)
+    g_all[c * n + a] = sum_slots(g_mid, n)
+    gather_send(g_all, G3)
     groups = rank // 8
     wait_many(gram, nx - 1, GRAM)
     whole = sum_slots(gram, nx)
@@ -416,34 +428,26 @@
     whole = jnp.where(eye_c == eye_r + rank, 1.0, whole)
     for g in range(groups):
         chol[g] = whole[8 * g : 8 * g + 8]
-    eliminate(chol, 0, groups // 4)
-    s_x[nx - 1] = part_sum(nx - 1)
-    s_xin[x * n + b] = s_x[nx - 1]
-
-    @functools.partial(each, n - 1)
-    def _(k):
-        j = wrap(b + far_first(k, n), n)
-        remote(s_x.at[nx - 1], s_xin.at[x * n + b], XX, at_b(j)).start()
-
-    wait_many(g_mid, n - 1, G2)
-    g_all[c * n + a] = sum_slots(g_mid, n)
-    gather_send(g_all, G3)
-    eliminate(chol, groups // 4, 5 * groups // 8)
+    eliminate(chol, 0, groups // 2, 0)
+    eliminate(chol, groups // 2, 5 * groups // 8, groups // 2)
 
     wait_many(s_xin, nx * n - 1, XX)
     s_all[c * n + a] = sum_slots(s_xin, nx * n)
     gather_send(s_all, C5)
-    eliminate(chol, 5 * groups // 8, groups)
-    inverse = unscaled_to_inverse([chol[g] for g in range(groups)], rank)[:, :rank]
-    basis_o[...] = lax.dot_general(inverse, left, NN, precision=HIGHEST, preferred_element_type=F32)
+    eliminate(chol, 5 * groups // 8, groups, groups // 2)
+    turned = [pltpu.roll(chol[g], 128 - rank // 2, 1) for g in range(groups // 2)]
+    turned += [chol[g] for g in range(groups // 2, groups)]
+    inverse = unscaled_to_inverse(turned, rank)[:, :rank]
+    inv_high = inverse.astype(BF16)
+    inv_low = (inverse - inv_high.astype(F32)).astype(BF16)
+    inv_stack = jnp.concatenate([inv_high, inv_high, inv_low], axis=1)
+    basis_o[...] = lax.dot_general(
+        inv_stack, jnp.concatenate([high, low, high], axis=0), NN, preferred_element_type=F32
+    )
     wait_many(g_all, pairs - 1, G3)
     gates = jnp.concatenate([g_all[k] for k in range(pairs)], axis=0)
     gate_o[...] = gates[:, :share]
     hist_o[...] = jnp.sum(gates[:, share:], axis=1, keepdims=True).T * hist_scale
-    inv_high = inverse.astype(BF16)
-    inv_low = (inverse - inv_high.astype(F32)).astype(BF16)
-    inv_stack = jnp.concatenate([inv_high, inv_high, inv_low], axis=1)
-
     wait_many(l_src, pairs - 1, A1, False)
     wait_many(t_src, nx - 1, TG, False)
     wait_many(l_mid, n - 1, A2, False)

time: 49.1 us -> 49.8 us (1.014)
  Pallas kernels: 48.4 us -> 49 us
    pallas_call x1, Pallas kernels: 47.5 us -> 48.1 us  [per_device(): pl.pallas_call(functools.partial(main_kernel, n, nx, workers, nbins / (to...]
where the time goes in v4:
time: 49.8 us; the launch traced here: 49.6 us
  Pallas kernels  49 us (98%)
  between operations  0.64 us (1%)
    pallas_call x1, Pallas kernels, per_device(): pl.pallas_call(functools.partial(main_kernel, n, nx, workers, nbins / (to...  48.1 us

profile of v4, /device:TPU:1, one launch (start us, length us, event | category | flops | bytes accessed | tf_op | source)
XLA Modules:
  0.0 49.6 jit_solution(706920307110150942)
XLA Ops:
  0.6 48.1 %main.1 = (f32[64,384]{1,0:T(8,128)S(1)}, f32[64,384]{1,0:T(8,128)S(1)}, f32[64,384]{1,0:T(8,128)S(1)}, f32[1,64]{1,0:T(1,128)S(1)}, bf16[384,384]{1,0:T(8,128)(2,1)S(1)}) custom-call(s32[3]{0:T(128)} %tb_hbm.1, f32[64]{0:T(128)} %sw_hbm.1, bf16[384,384]{1,0:T(8,128)(2,1)} %head_hbm.1, bf16[384,1536]{1,0:T(8,128)(2,1)} %weight_hbm.1, ...), custom_call_target="tpu_custom_call" | custom-call | tf_op jit(solution)/shard_map/main/pallas_call | solution.py:516
  48.8 0.9 %finish.1 = (f32[64,384]{1,0:T(8,128)}, f32[64,384]{1,0:T(8,128)}, f32[64,384]{1,0:T(8,128)}, f32[1,64]{1,0:T(1,128)}, bf16[384,384]{1,0:T(8,128)(2,1)}) custom-call(f32[64,384]{1,0:T(8,128)S(1)} %get-tuple-element.15.refs_0_, f32[64,384]{1,0:T(8,128)S(1)} %get-tuple-element.16.refs_1_, f32[64,384]{1,0:T(8,128)S(1)} %get-tuple-element.17.refs_2_, ...), custom_call_target="tpu_custom_call" | custom-call | tf_op jit(solution)/shard_map/finish/pallas_call | solution.py:566

commit v5 on v4

--- a/solution.py
+++ b/solution.py
@@ -398,28 +398,6 @@
         remote(gram.at[x], gram.at[x], GRAM, (index, target(i))).start()
 
     each(nx, part_scatter)
-
-
-    @functools.partial(each, nx - 1)
-    def _(i):
-        s_x[i] = part_sum(i)
-
-        @functools.partial(each, n)
-        def _(k):
-            j = wrap(b + far_first(k, n), n)
-            remote(s_x.at[i], s_xin.at[x * n + b], XX, at_b(j, target(i))).start()
-
-    s_x[nx - 1] = part_sum(nx - 1)
-    s_xin[x * n + b] = s_x[nx - 1]
-
-    @functools.partial(each, n - 1)
-    def _(k):
-        j = wrap(b + far_first(k, n), n)
-        remote(s_x.at[nx - 1], s_xin.at[x * n + b], XX, at_b(j)).start()
-
-    wait_many(g_mid, n - 1, G2)
-    g_all[c * n + a] = sum_slots(g_mid, n)
-    gather_send(g_all, G3)
     groups = rank // 8
     wait_many(gram, nx - 1, GRAM)
     whole = sum_slots(gram, nx)
@@ -428,7 +406,29 @@
     whole = jnp.where(eye_c == eye_r + rank, 1.0, whole)
     for g in range(groups):
         chol[g] = whole[8 * g : 8 * g + 8]
-    eliminate(chol, 0, groups // 2, 0)
+    eliminate(chol, 0, groups // 4, 0)
+
+    @functools.partial(each, nx - 1)
+    def _(i):
+        s_x[i] = part_sum(i)
+
+        @functools.partial(each, n)
+        def _(k):
+            j = wrap(b + far_first(k, n), n)
+            remote(s_x.at[i], s_xin.at[x * n + b], XX, at_b(j, target(i))).start()
+
+    s_x[nx - 1] = part_sum(nx - 1)
+    s_xin[x * n + b] = s_x[nx - 1]
+
+    @functools.partial(each, n - 1)
+    def _(k):
+        j = wrap(b + far_first(k, n), n)
+        remote(s_x.at[nx - 1], s_xin.at[x * n + b], XX, at_b(j)).start()
+
+    wait_many(g_mid, n - 1, G2)
+    g_all[c * n + a] = sum_slots(g_mid, n)
+    gather_send(g_all, G3)
+    eliminate(chol, groups // 4, groups // 2, 0)
     eliminate(chol, groups // 2, 5 * groups // 8, groups // 2)
 
     wait_many(s_xin, nx * n - 1, XX)

time: 49.8 us -> 50.4 us (1.012)
  Pallas kernels: 49 us -> 49.6 us
    pallas_call x1, Pallas kernels: 48.1 us -> 48.7 us  [per_device(): pl.pallas_call(functools.partial(main_kernel, n, nx, workers, nbins / (to...]
where the time goes in v5:
time: 50.4 us; the launch traced here: 50.2 us
  Pallas kernels  49.6 us (98%)
  between operations  0.64 us (1%)
    pallas_call x1, Pallas kernels, per_device(): pl.pallas_call(functools.partial(main_kernel, n, nx, workers, nbins / (to...  48.7 us

profile of v5, /device:TPU:1, one launch (start us, length us, event | category | flops | bytes accessed | tf_op | source)
XLA Modules:
  0.0 50.2 jit_solution(5823502169987432743)
XLA Ops:
  0.6 48.7 %main.1 = (f32[64,384]{1,0:T(8,128)S(1)}, f32[64,384]{1,0:T(8,128)S(1)}, f32[64,384]{1,0:T(8,128)S(1)}, f32[1,64]{1,0:T(1,128)S(1)}, bf16[384,384]{1,0:T(8,128)(2,1)S(1)}) custom-call(s32[3]{0:T(128)} %tb_hbm.1, f32[64]{0:T(128)} %sw_hbm.1, bf16[384,384]{1,0:T(8,128)(2,1)} %head_hbm.1, bf16[384,1536]{1,0:T(8,128)(2,1)} %weight_hbm.1, ...), custom_call_target="tpu_custom_call" | custom-call | tf_op jit(solution)/shard_map/main/pallas_call | solution.py:516
  49.4 0.9 %finish.1 = (f32[64,384]{1,0:T(8,128)}, f32[64,384]{1,0:T(8,128)}, f32[64,384]{1,0:T(8,128)}, f32[1,64]{1,0:T(1,128)}, bf16[384,384]{1,0:T(8,128)(2,1)}) custom-call(f32[64,384]{1,0:T(8,128)S(1)} %get-tuple-element.15.refs_0_, f32[64,384]{1,0:T(8,128)S(1)} %get-tuple-element.16.refs_1_, f32[64,384]{1,0:T(8,128)S(1)} %get-tuple-element.17.refs_2_, ...), custom_call_target="tpu_custom_call" | custom-call | tf_op jit(solution)/shard_map/finish/pallas_call | solution.py:566
